TPU v7x, 32 devices: a whole 2x2x4 slice. The times are simulated.
32 devices in a mesh: grp: 4 (over y, core), orb: 8 (over z, x).
Axes of the slice: x: 2, y: 2, z: 4, core: 2. Of those that a mesh axis runs over, the one named last changes fastest.
Arguments:
- slabs: float32 [32, 256, 1024], P(('grp', 'orb')), may hold values from -0.9 to 0.9
- eps_occ: float32 [32], P(('grp', 'orb')), may hold values from -1.5 to -0.5
- eps_vir: float32 [256], replicated, may hold values from 0.2 to 3
Outputs:
- gradient: float32 [32, 256, 1024], P(('grp', 'orb'))
- density: float32 [256, 256], P('orb')
All inputs are finite; a program needn't handle non-finite values.
Results may differ from a plain program's by a relative error of at most 0.0003.
Values sent between devices are 32-bit elements; how exact they have to be, the bound alone decides.
A program may use at most 64 MiB of HBM per device.

v0:
```python
import jax
import jax.numpy as jnp
from jax import lax
from jax.sharding import PartitionSpec as P


def partner(value, axis, bit):
    mask = 2**bit
    pairs = [(source, source ^ mask) for source in range(lax.axis_size(axis))]
    return lax.ppermute(value, axis, pairs)


def pair_terms(own, other, e_own, e_other, eps_vir):
    coulomb = jnp.dot(
        own, other.T, precision=lax.Precision.HIGHEST, preferred_element_type=jnp.float32
    )
    denom = e_own + e_other - eps_vir[:, None] - eps_vir[None, :]
    amps = coulomb / denom
    spin = 2.0 * amps - amps.T
    grad = jnp.dot(spin, other, precision=lax.Precision.HIGHEST, preferred_element_type=jnp.float32)
    dens = jnp.dot(
        amps, spin.T, precision=lax.Precision.HIGHEST, preferred_element_type=jnp.float32
    )
    return (grad, dens)


def per_device(slabs, eps_occ, eps_vir):
    own = slabs[0]
    e_own = eps_occ[0]
    first_slab, first_energy = partner((own, eps_occ), "orb", 0)
    second_slab, second_energy = partner((own, eps_occ), "orb", 1)
    third_slab, third_energy = partner((first_slab, first_energy), "orb", 1)
    partners = (
        (first_slab, first_energy),
        (second_slab, second_energy),
        (third_slab, third_energy),
    )
    gradient = jnp.zeros(own.shape, jnp.float32)
    rows = own.shape[0] // lax.axis_size("orb")
    share = jnp.zeros((rows, own.shape[0]), jnp.float32)
    for other, e_other in partners:
        g_part, d_part = pair_terms(own, other, e_own, e_other[0], eps_vir)
        gradient = gradient + g_part
        share = share + lax.psum_scatter(d_part, "orb", scatter_dimension=0, tiled=True)
    total = lax.psum(share, "grp")
    count = lax.axis_size("grp") * lax.axis_size("orb")
    return (gradient[None], total / count)


def solution(mesh):
    placed = (P(("grp", "orb"), None, None), P(("grp", "orb")), P())
    return jax.shard_map(
        per_device,
        mesh=mesh,
        in_specs=placed,
        out_specs=(P(("grp", "orb"), None, None), P("orb", None)),
        check_vma=False,
    )
```

profile of v0, /device:TPU:0, one launch (start us, length us, event | category | flops | bytes accessed | tf_op | source)
XLA Modules:
  0.0 150.3 jit_solution(9536104641548881515)
XLA Ops:
  7.2 3.1 %collective-permute-start.2 = (f32[256,1024]{1,0:T(8,128)}, f32[256,1024]{1,0:T(8,128)S(1)}, u32[]{:S(2)}, u32[]{:S(2)}) collective-permute-start(f32[256,1024]{1,0:T(8,128)} %bitcast.36), channel_id=1, source_target_pairs={{0,2},{1,3},{2,0},{3,1},{4,6},{5,7},{6,4},{7,5},{8,10},{9,11},{10,... | collective-permute-start | bytes 3145736 | tf_op jit(solution)/shard_map/ppermute | solution.py:10
  10.3 1.5 collective-permute-start
  11.8 0.5 collective-permute-start.1
  13.1 22.2 %collective-permute-done.1 = f32[1]{0:T(128)} collective-permute-done((f32[1]{0:T(128)}, f32[1]{0:T(128)}, u32[]{:S(2)}, u32[]{:S(2)}) %collective-permute-start.1) | collective-permute-done | bytes 36 | tf_op jit(solution)/shard_map/ppermute | solution.py:10
  35.3 0.4 collective-permute-start.5
  37.0 2.0 %collective-permute-done.5 = f32[1]{0:T(128)} collective-permute-done((f32[1]{0:T(128)}, f32[1]{0:T(128)}, u32[]{:S(2)}, u32[]{:S(2)}) %collective-permute-start.5) | collective-permute-done | bytes 36 | tf_op jit(solution)/shard_map/ppermute | solution.py:10
  39.7 0.7 copy-done.5
  40.4 2.3 %fusion.7 = f32[256,256]{1,0:T(8,128)S(1)} fusion(f32[256,1024]{1,0:T(8,128)S(1)} %collective-permute-done.2, f32[1,256,1024]{2,1,0:T(8,128)} %param.3), kind=kOutput, calls=%fused_computation.21 | convolution fusion | flops 805306368 | bytes 2359296 | tf_op jit(solution)/shard_map/dot_general | solution.py:14
  42.9 0.4 collective-permute-start.4
  43.3 2.3 %fusion.9 = f32[256,256]{1,0:T(8,128)S(1)} fusion(f32[256,1024]{1,0:T(8,128)} %collective-permute-done, f32[1,256,1024]{2,1,0:T(8,128)S(1)} %copy-done), kind=kOutput, calls=%fused_computation.23 | convolution fusion | flops 805306368 | bytes 2359296 | tf_op jit(solution)/shard_map/dot_general | solution.py:14
  45.6 0.1 copy.5
  45.8 0.7 fusion.4
  46.5 1.4 convolution_add_fusion.3
  48.0 2.2 %fusion.12 = f32[256,1024]{1,0:T(8,128)S(1)} fusion(f32[256,1024]{1,0:T(8,128)S(1)} %collective-permute-done.2, f32[256,256]{1,0:T(8,128)} %copy-done.1, f32[256]{0:T(256)S(1)} %get-tuple-element.4, f32[256]{0:T(256)S(1)} %copy-done.5, f32[256,256]{0,1:T(8,128)} %copy-done.4), kind=kOutput, calls=%fused_computation.25 | convolution fusion | flops 805699584 | bytes 2623488 | tf_op jit(solution)/shard_map/dot_general | solution.py:20
  50.2 15.6 %collective-permute-done.4 = f32[256,1024]{1,0:T(8,128)} collective-permute-done((f32[256,1024]{1,0:T(8,128)}, f32[256,1024]{1,0:T(8,128)}, u32[]{:S(2)}, u32[]{:S(2)}) %collective-permute-start.4) | collective-permute-done | bytes 1048608 | tf_op jit(solution)/shard_map/ppermute | solution.py:10
  65.8 2.3 %fusion.5 = f32[256,256]{1,0:T(8,128)S(1)} fusion(f32[256,1024]{1,0:T(8,128)} %collective-permute-done.4, f32[1,256,1024]{2,1,0:T(8,128)S(1)} %copy-done), kind=kOutput, calls=%fused_computation.19 | convolution fusion | flops 805306368 | bytes 2359296 | tf_op jit(solution)/shard_map/dot_general | solution.py:14
  68.2 0.8 copy-done.6
  69.0 1.4 convolution_add_fusion.2
  70.5 0.9 copy-done.3
  71.4 2.4 %convolution_add_fusion.1 = f32[256,1024]{1,0:T(8,128)S(1)} fusion(f32[256,1024]{1,0:T(8,128)S(1)} %fusion.12, f32[256,1024]{1,0:T(8,128)} %collective-permute-done, f32[256,256]{1,0:T(8,128)S(1)} %fusion.9, f32[256]{0:T(256)S(1)} %copy-done.5, f32[256]{0:T(256)S(1)} %get-tuple-element.3, f32[256,256]{0,1:T(8,128)S(1)} %copy-done.3), kind=kOutput, calls=%fused_computation.2 | convolution fusion | flops 805961728 | bytes 3672064 | tf_op jit(solution)/shard_map/dot_general | solution.py:20
  73.8 3.4 %fusion = f32[1,256,1024]{2,1,0:T(8,128)} fusion(f32[256,1024]{1,0:T(8,128)S(1)} %convolution_add_fusion.1, f32[256,1024]{1,0:T(8,128)} %collective-permute-done.4, f32[256,256]{1,0:T(8,128)S(1)} %fusion.5, f32[256]{0:T(256)S(1)} %get-tuple-element.2, f32[256]{0:T(256)S(1)} %copy-done.5, f32[256,256]{0,1:T(8,128)S(1)} %copy.7), kind=kOutput, calls=%fused_computation.1 | convolution fusion | flops 805961728 | bytes 3672064 | tf_op jit(solution)/shard_map/dot_general | solution.py:20
  77.1 54.9 %reduce-scatter.2.cloned.1.call-done = f32[32,256]{1,0:T(8,128)} async-done(((f32[256,256]{1,0:T(8,128)}), f32[32,256]{1,0:T(8,128)}) %reduce-scatter.2.cloned.1.call-update) | async-done | bytes 32784 | tf_op jit(solution)/shard_map/reduce_scatter | solution.py:44
  132.1 10.8 %psum.7 = f32[32,256]{1,0:T(8,128)S(1)} all-reduce(f32[32,256]{1,0:T(8,128)} %reduce-scatter.2.cloned.1.call-done), channel_id=1, replica_groups=mesh['grp'=4,'orb'=8] {'grp'}, use_global_device_ids=true, to_apply=%region_3.0 | all-reduce | flops 8192 | bytes 65536 | tf_op jit(solution)/shard_map/psum | solution.py:45
  142.9 0.6 broadcast_multiply_fusion
  (20 shorter events, 0.4 us)
Async XLA Ops:
  7.2 124.9 %reduce-scatter.2.cloned.1.call-start = ((), (), s32[]{:S(2)}) async-start(), calls=%async_computation.1 | async-start | bytes 294912 | tf_op jit(solution)/shard_map/reduce_scatter | solution.py:44
  7.2 33.2 %collective-permute-start.2 = (f32[256,1024]{1,0:T(8,128)}, f32[256,1024]{1,0:T(8,128)S(1)}, u32[]{:S(2)}, u32[]{:S(2)}) collective-permute-start(f32[256,1024]{1,0:T(8,128)} %bitcast.36), channel_id=1, source_target_pairs={{0,2},{1,3},{2,0},{3,1},{4,6},{5,7},{6,4},{7,5},{8,10},{9,11},{10,... | collective-permute-start | bytes 3145736 | tf_op jit(solution)/shard_map/ppermute | solution.py:10
  10.3 32.6 %collective-permute-start = (f32[256,1024]{1,0:T(8,128)}, f32[256,1024]{1,0:T(8,128)}, u32[]{:S(2)}, u32[]{:S(2)}) collective-permute-start(f32[256,1024]{1,0:T(8,128)} %bitcast.37), channel_id=1, source_target_pairs={{0,1},{1,0},{2,3},{3,2},{4,5},{5,4},{6,7},{7,6},{8,9},{9,8},{10,11... | collective-permute-start | bytes 3145736 | tf_op jit(solution)/shard_map/ppermute | solution.py:10
  11.8 23.5 %collective-permute-start.1 = (f32[1]{0:T(128)}, f32[1]{0:T(128)}, u32[]{:S(2)}, u32[]{:S(2)}) collective-permute-start(f32[1]{0:T(128)} %param.4), channel_id=1, source_target_pairs={{0,1},{1,0},{2,3},{3,2},{4,5},{5,4},{6,7},{7,6},{8,9},{9,8},{10,11... | collective-permute-start | bytes 20 | tf_op jit(solution)/shard_map/ppermute | solution.py:10
  12.3 23.9 %collective-permute-start.3 = (f32[1]{0:T(128)}, f32[1]{0:T(128)}, u32[]{:S(2)}, u32[]{:S(2)}) collective-permute-start(f32[1]{0:T(128)} %param.4), channel_id=1, source_target_pairs={{0,2},{1,3},{2,0},{3,1},{4,6},{5,7},{6,4},{7,5},{8,10},{9,11},{10,... | collective-permute-start | bytes 20 | tf_op jit(solution)/shard_map/ppermute | solution.py:10
  35.3 3.7 %collective-permute-start.5 = (f32[1]{0:T(128)}, f32[1]{0:T(128)}, u32[]{:S(2)}, u32[]{:S(2)}) collective-permute-start(f32[1]{0:T(128)} %collective-permute-done.1), channel_id=1, source_target_pairs={{0,2},{1,3},{2,0},{3,1},{4,6},{5,7},{6,4},{7,5},{8,10},{9,11},{10,... | collective-permute-start | bytes 20 | tf_op jit(solution)/shard_map/ppermute | solution.py:10
  39.7 0.7 copy-start.5
  40.4 3.0 %copy-start = (f32[1,256,1024]{2,1,0:T(8,128)S(1)}, f32[1,256,1024]{2,1,0:T(8,128)}, u32[]{:S(2)}) copy-start(f32[1,256,1024]{2,1,0:T(8,128)} %param.3) | copy-start | bytes 3145732
  42.7 3.8 %copy-start.1 = (f32[256,256]{1,0:T(8,128)}, f32[256,256]{1,0:T(8,128)S(1)}, u32[]{:S(2)}) copy-start(f32[256,256]{1,0:T(8,128)S(1)} %fusion.7) | copy-start | bytes 786436
  42.9 3.7 %copy-start.4 = (f32[256,256]{0,1:T(8,128)}, f32[256,256]{0,1:T(8,128)S(1)}, u32[]{:S(2)}) copy-start(f32[256,256]{0,1:T(8,128)S(1)} %copy.6) | copy-start | bytes 786436
  42.9 22.9 %collective-permute-start.4 = (f32[256,1024]{1,0:T(8,128)}, f32[256,1024]{1,0:T(8,128)}, u32[]{:S(2)}, u32[]{:S(2)}) collective-permute-start(f32[256,1024]{1,0:T(8,128)} %collective-permute-done), channel_id=1, source_target_pairs={{0,2},{1,3},{2,0},{3,1},{4,6},{5,7},{6,4},{7,5},{8,10},{9,11},{10,... | collective-permute-start | bytes 3145736 | tf_op jit(solution)/shard_map/ppermute | solution.py:10
  45.8 0.7 copy-start.2
  68.1 1.0 copy-start.6
  70.4 0.9 copy-start.3
Sparse Core Ops, SparseCore 0:
  70.6 61.4 reduce-scatter.1
where the time goes:
time: 151 us; the launch traced here: 150 us
  waiting for transfers between devices  94.8 us (63%)
  matrix products  18.4 us (12%)
  between operations  16.9 us (11%)
  blocking collectives  10.8 us (7%)
  starting transfers between devices  6.02 us (4%)
  local copies, waits for them, and re-layouts  2.81 us (2%)
    reduce_scatter x1, waiting for transfers between devices, per_device(): lax.psum_scatter(d_part, 'orb', scatter_dimension=0, tiled=True)  54.9 us
    ppermute x6, waiting for transfers between devices, partner(): return lax.ppermute(value, axis, pairs)  39.8 us
    psum x1, blocking collectives, per_device(): total = lax.psum(share, 'grp')  10.8 us
    dot_general x3, matrix products, pair_terms(): jnp.dot(spin, other, precision=lax.Precision.HIGHEST, preferred_element_t...  7.95 us
    dot_general x3, matrix products, pair_terms(): jnp.dot(own, other.T, precision=lax.Precision.HIGHEST, preferred_element_...  6.9 us
    ppermute x6, starting transfers between devices, partner(): return lax.ppermute(value, axis, pairs)  5.98 us
    dot_general x3, matrix products, pair_terms(): jnp.dot(amps, spin.T, precision=lax.Precision.HIGHEST, preferred_element_...  3.59 us
  transfers between devices with their start and end apart: 7, of which 4 were waited for; matrix products, arithmetic and copies ran while one was open for 10% of the time, Pallas kernels for 0%

commit v1 on v0

v1 whole, which is shorter than its diff:
```python
import functools

import jax
import jax.numpy as jnp
from jax import lax
from jax.experimental import pallas as pl
from jax.experimental.pallas import tpu as pltpu
from jax.sharding import PartitionSpec as P

MESH = pl.DeviceIdType.MESH
F32, BF16 = jnp.float32, jnp.bfloat16
CHUNKS = 4


def nt(a, b):
    return lax.dot_general(a, b, (((1,), (1,)), ((), ())), preferred_element_type=F32)


def nn(a, b):
    return lax.dot_general(a, b, (((1,), (0,)), ((), ())), preferred_element_type=F32)


def split(value):
    high = value.astype(BF16)
    return high, (value - high.astype(F32)).astype(BF16)


def product(dot, a, b):
    return dot(a[0], b[0]) + (dot(a[0], b[1]) + dot(a[1], b[0]))


def kernel(
    fused, n_grp, n_orb,
    eps_ref, vir_ref, slab_ref, grad_ref, dens_ref,
    own_hi, own_lo, own, xs, xs_hi, xs_lo, zs, zs_hi, zs_lo, ds, ds_hi, ds_lo,
    level, energy, part, from_grp, summed, from_orb, final, rows_out,
    own_sem, x_sem, z_sem, fx_sem, fz_sem, e_sem, g_sem, o_sem, h_sem,
):
    virt, naux = own.shape
    width = naux // CHUNKS
    half = CHUNKS // 2
    grp, orb = lax.axis_index("grp"), lax.axis_index("orb")
    x_id = orb + 1 - 2 * lax.rem(orb, 2)
    z_id = orb + 2 - 4 * lax.rem(orb // 2, 2)
    d_id = x_id + z_id - orb

    load = pltpu.make_async_copy(slab_ref, own, own_sem)
    load.start()

    barrier = pltpu.get_barrier_semaphore()
    greeted = 0
    if fused:
        for r in range(1, n_grp):
            pl.semaphore_signal(
                barrier, inc=1, device_id={"grp": lax.rem(grp + r, n_grp)}, device_id_type=MESH
            )
        for r in range(1, n_orb):
            pl.semaphore_signal(
                barrier, inc=1, device_id={"orb": lax.rem(orb + r, n_orb)}, device_id_type=MESH
            )
        greeted = n_grp + n_orb - 2
    else:
        for to in (x_id, z_id, d_id):
            pl.semaphore_signal(barrier, inc=1, device_id={"orb": to}, device_id_type=MESH)
        greeted = 3
    energy[3] = jnp.full(energy.shape[1:], eps_ref[0], F32)
    pl.semaphore_wait(barrier, greeted)

    def remote(src, dst, sems, slot, **to):
        return pltpu.make_async_remote_copy(
            src_ref=src, dst_ref=dst, send_sem=sems.at[0, slot], recv_sem=sems.at[1, slot],
            device_id=to, device_id_type=MESH,
        )

    def cols(c):
        return (slice(None), pl.ds(c * width, width))

    x_copy = [remote(slab_ref.at[cols(c)], xs.at[cols(c)], x_sem, c, orb=x_id) for c in range(CHUNKS)]
    z_copy = [remote(slab_ref.at[cols(c)], zs.at[cols(c)], z_sem, c, orb=z_id) for c in range(CHUNKS)]
    fx_copy = [remote(zs.at[cols(c)], ds.at[cols(c)], fx_sem, c, orb=x_id) for c in range(half)]
    fz_copy = [
        remote(xs.at[cols(c + half)], ds.at[cols(c + half)], fz_sem, c, orb=z_id) for c in range(half)
    ]
    e_copy = [
        remote(energy.at[3], energy.at[s], e_sem, s, orb=to) for s, to in enumerate((x_id, z_id, d_id))
    ]
    for copy in e_copy:
        copy.start()
    for s in range(CHUNKS):
        x_copy[(s + half) % CHUNKS].start()
        z_copy[s].start()

    row = jnp.broadcast_to(vir_ref[...][None, :], (virt, virt))
    level[...] = row + row.T
    load.wait()
    own_hi[...], own_lo[...] = split(own[...])

    def ref_pair(hi, lo, c):
        return hi[cols(c)], lo[cols(c)]

    def take(src, hi, lo, c):
        hi[cols(c)], lo[cols(c)] = split(src[cols(c)])

    def coulomb(a, b, c):
        return product(nt, ref_pair(*a, c), ref_pair(*b, c))

    mine, firsts, seconds, thirds = (own_hi, own_lo), (xs_hi, xs_lo), (zs_hi, zs_lo), (ds_hi, ds_lo)
    k_x = k_z = jnp.zeros((virt, virt), F32)
    for s in range(CHUNKS):
        c = (s + half) % CHUNKS
        x_copy[c].wait_recv()
        take(xs, *firsts, c)
        z_copy[s].wait_recv()
        take(zs, *seconds, s)
        if s == CHUNKS - 2:
            for f in range(half):
                fx_copy[f].start()
                fz_copy[f].start()
        k_x = k_x + coulomb(mine, firsts, c)
        k_z = k_z + coulomb(mine, seconds, s)
    k_xz = jnp.zeros((virt, virt), F32)
    for c in range(CHUNKS):
        k_xz = k_xz + coulomb(firsts, seconds, c)
    for copy in e_copy:
        copy.wait_recv()
    e_x, e_z, e_d, e_own = (energy[s][:1, :1] for s in range(4))

    def amplitudes(k, energies):
        amps = k / (energies - level[...])
        return amps, 2.0 * amps - amps.T

    t_x, s_x = amplitudes(k_x, e_own + e_x)
    t_z, s_z = amplitudes(k_z, e_own + e_z)
    t_xz, s_xz = amplitudes(k_xz, e_x + e_z)
    s_x, s_z = split(s_x), split(s_z)
    density = (
        product(nt, split(t_x), s_x)
        + product(nt, split(t_z), s_z)
        + product(nt, split(t_xz), split(s_xz))
    )

    def gradient(spin, src, c):
        return product(nn, spin, ref_pair(*src, c))

    waits = []
    if fused:
        part[...] = density.reshape(part.shape)
        g_copy = [
            remote(part.at[:, lax.rem(grp + r, n_grp)], from_grp.at[r - 1], g_sem, r - 1,
                   grp=lax.rem(grp + r, n_grp))
            for r in range(1, n_grp)
        ]
        for copy in g_copy:
            copy.start()
    else:
        dens_ref[...] = density

    for c in range(CHUNKS):
        grad_ref[cols(c)] = gradient(s_x, firsts, c)

    if fused:
        for copy in g_copy:
            copy.wait_recv()
        total = part[:, pl.ds(grp, 1)][:, 0]
        for r in range(n_grp - 1):
            total = total + from_grp[r]
        summed[...] = total
        o_copy = [
            remote(summed.at[lax.rem(orb + r, n_orb)], from_orb.at[r - 1], o_sem, r - 1,
                   orb=lax.rem(orb + r, n_orb))
            for r in range(1, n_orb)
        ]
        for copy in o_copy:
            copy.start()
        waits += g_copy + o_copy

    for c in range(CHUNKS):
        grad_ref[cols(c)] += gradient(s_z, seconds, c)

    if fused:
        for copy in o_copy:
            copy.wait_recv()
        total = summed[pl.ds(orb, 1)][0]
        for r in range(n_orb - 1):
            total = total + from_orb[r]
        final[...] = total * (1.0 / (n_grp * n_orb))
        h_copy = [
            remote(final, rows_out.at[r - 1], h_sem, r - 1, grp=lax.rem(grp + r, n_grp))
            for r in range(1, n_grp)
        ]
        for copy in h_copy:
            copy.start()
        waits += h_copy

    k_d = jnp.zeros((virt, virt), F32)
    for f in range(half):
        for copy, c in ((fx_copy[f], f), (fz_copy[f], f + half)):
            copy.wait_recv()
            take(ds, *thirds, c)
            k_d = k_d + coulomb(mine, thirds, c)
    _, s_d = amplitudes(k_d, e_own + e_d)
    s_d = split(s_d)
    for c in range(CHUNKS):
        grad_ref[cols(c)] += gradient(s_d, thirds, c)

    if fused:
        block = final.shape[0]
        dens_ref[pl.ds(pl.multiple_of(grp * block, block), block), :] = final[...]
        for r in range(1, n_grp):
            h_copy[r - 1].wait_recv()
            at = lax.rem(grp + (n_grp - r), n_grp)
            dens_ref[pl.ds(pl.multiple_of(at * block, block), block), :] = rows_out[r - 1]
    for copy in x_copy + z_copy + fx_copy + fz_copy + e_copy + waits:
        copy.wait_send()


def per_device(slabs, eps_occ, eps_vir):
    own = slabs[0]
    virt, naux = own.shape
    n_grp, n_orb = lax.axis_size("grp"), lax.axis_size("orb")
    rows = virt // n_orb
    block = rows // n_grp
    fused = rows % n_grp == 0 and block % 8 == 0
    if not fused:
        block = 8
    whole = (virt, naux)
    wide = [pltpu.VMEM(whole, BF16)] * 2
    dma = lambda count: pltpu.SemaphoreType.DMA((2, count))
    gradient, density = pl.pallas_call(
        functools.partial(kernel, fused, n_grp, n_orb),
        out_shape=(
            jax.ShapeDtypeStruct(whole, F32),
            jax.ShapeDtypeStruct((rows if fused else virt, virt), F32),
        ),
        in_specs=[
            pl.BlockSpec(memory_space=pltpu.SMEM),
            pl.BlockSpec(memory_space=pltpu.VMEM),
            pl.BlockSpec(memory_space=pl.ANY),
        ],
        out_specs=(pl.BlockSpec(memory_space=pltpu.VMEM),) * 2,
        scratch_shapes=[
            *wide,
            pltpu.VMEM(whole, F32),
            *([pltpu.VMEM(whole, F32), *wide] * 3),
            pltpu.VMEM((virt, virt), F32),
            pltpu.VMEM((4, 8, 128), F32),
            pltpu.VMEM((n_orb, n_grp, block, virt), F32),
            pltpu.VMEM((n_grp - 1, n_orb, block, virt), F32),
            pltpu.VMEM((n_orb, block, virt), F32),
            pltpu.VMEM((n_orb - 1, block, virt), F32),
            pltpu.VMEM((block, virt), F32),
            pltpu.VMEM((n_grp - 1, block, virt), F32),
            pltpu.SemaphoreType.DMA,
            dma(CHUNKS), dma(CHUNKS), dma(CHUNKS // 2), dma(CHUNKS // 2), dma(3),
            dma(n_grp - 1), dma(n_orb - 1), dma(n_grp - 1),
        ],
        compiler_params=pltpu.CompilerParams(
            collective_id=0, has_side_effects=True, vmem_limit_bytes=40 * 2**20
        ),
        cost_estimate=pl.CostEstimate(
            flops=18 * virt * virt * (2 * naux + virt), bytes_accessed=8 * virt * naux, transcendentals=0
        ),
    )(eps_occ, eps_vir, own)
    if not fused:
        share = lax.psum_scatter(density, "orb", scatter_dimension=0, tiled=True)
        density = lax.psum(share, "grp") / (n_grp * n_orb)
    return gradient[None], density


def solution(mesh):
    placed = (P(("grp", "orb"), None, None), P(("grp", "orb")), P())
    return jax.shard_map(
        per_device,
        mesh=mesh,
        in_specs=placed,
        out_specs=(P(("grp", "orb"), None, None), P("orb", None)),
        check_vma=False,
    )
```

time: 151 us -> 50.7 us (0.34)
  waiting for transfers between devices: 94.8 us -> 0 us
  Pallas kernels: 0 us -> 45.8 us
  matrix products: 18.4 us -> 0 us
  between operations: 16.9 us -> 1.29 us
  blocking collectives: 10.8 us -> 0 us
  starting transfers between devices: 6.02 us -> 0 us
    reduce_scatter x1 -> x0, waiting for transfers between devices: 54.9 us -> none  [per_device(): lax.psum_scatter(d_part, 'orb', scatter_dimension=0, tiled=True)]
    pallas_call x0 -> x1, Pallas kernels: none -> 45.8 us  [per_device(): pl.pallas_call(functools.partial(kernel, fused, n_grp, n_orb), out_shape=...]
    ppermute x6 -> x0, waiting for transfers between devices: 39.8 us -> none  [partner(): return lax.ppermute(value, axis, pairs)]
    dot_general x9 -> x0, matrix products: 18.4 us -> none  [the longest x3 7.95 us: pair_terms(): jnp.dot(spin, other, precision=lax.Precision.HIGHEST, preferred_element_t...]
    psum x1 -> x0, blocking collectives: 10.8 us -> none  [per_device(): total = lax.psum(share, 'grp')]
    ppermute x6 -> x0, starting transfers between devices: 5.98 us -> none  [partner(): return lax.ppermute(value, axis, pairs)]
    unnamed x14 -> x6, local copies, waits for them, and re-layouts: 2.42 us -> 3.48 us
  transfers between devices with their start and end apart: 7 -> 0, of which waited for: 4 -> 0; matrix products, arithmetic and copies ran while one was open for 10% -> 0% of each run, Pallas kernels for 0% -> 0%
where the time goes in v1:
time: 50.7 us; the launch traced here: 50.6 us
  Pallas kernels  45.8 us (90%)
  local copies, waits for them, and re-layouts  3.48 us (7%)
  between operations  1.29 us (3%)
    pallas_call x1, Pallas kernels, per_device(): pl.pallas_call(functools.partial(kernel, fused, n_grp, n_orb), out_shape=...  45.8 us
    unnamed x6, local copies, waits for them, and re-layouts  3.48 us

profile of v1, /device:TPU:0, one launch (start us, length us, event | category | flops | bytes accessed | tf_op | source)
XLA Modules:
  0.0 50.6 jit_solution(12783522335628033624)
XLA Ops:
  1.3 0.0 copy-start.1
  1.3 0.7 %copy-done.1 = f32[256]{0:T(256)S(1)} copy-done((f32[256]{0:T(256)S(1)}, f32[256]{0:T(256)}, u32[]{:S(2)}) %copy-start.1) | copy-done | bytes 1048
  2.0 0.0 copy-start
  2.0 1.2 %copy-done = f32[1,256,1024]{2,1,0:T(8,128)S(1)} copy-done((f32[1,256,1024]{2,1,0:T(8,128)S(1)}, f32[1,256,1024]{2,1,0:T(8,128)}, u32[]{:S(2)}) %copy-start) | copy-done | bytes 1048600
  3.2 45.8 %shard_map.50 = (f32[256,1024]{1,0:T(8,128)S(1)}, f32[32,256]{1,0:T(8,128)S(1)}) custom-call(f32[1]{0:T(128)S(6)} %copy.7.eps_ref, f32[256]{0:T(256)S(1)} %copy-done.1, f32[256,1024]{1,0:T(8,128)S(1)} %bitcast.3), custom_call_target="tpu_custom_call" | custom-call | flops 2717908992 | bytes 2097152 | tf_op jit(solution)/shard_map/pallas_call | solution.py:229
  49.0 1.0 %copy.8 = f32[1,256,1024]{2,1,0:T(8,128)} copy(f32[1,256,1024]{2,1,0:T(8,128)S(1)} %bitcast.2) | data formatting | bytes 2097152
  49.9 0.6 %copy.9 = f32[32,256]{1,0:T(8,128)} copy(f32[32,256]{1,0:T(8,128)S(1)} %get-tuple-element.9) | data formatting | bytes 65536
Async XLA Ops:
  1.3 0.7 %copy-start.1 = (f32[256]{0:T(256)S(1)}, f32[256]{0:T(256)}, u32[]{:S(2)}) copy-start(f32[256]{0:T(256)} %vir_ref.1) | copy-start | bytes 3076
  2.0 1.2 %copy-start = (f32[1,256,1024]{2,1,0:T(8,128)S(1)}, f32[1,256,1024]{2,1,0:T(8,128)}, u32[]{:S(2)}) copy-start(f32[1,256,1024]{2,1,0:T(8,128)} %param.3) | copy-start | bytes 3145732
